TPU v7x, 32 devices: a whole 2x2x4 slice. The times are simulated.
32 devices in a mesh: ctx: 8 (over z, y), tp: 4 (over x, core).
Axes of the slice: x: 2, y: 2, z: 4, core: 2. Of those that a mesh axis runs over, the one named last changes fastest.
Arguments:
- query_proj: bfloat16 [2048, 8192], P('ctx', 'tp'), may hold values from -24 to 24, as said below
- key_proj: bfloat16 [2048, 8192], P('ctx', 'tp'), may hold values from -6 to 6
- value_proj: bfloat16 [2048, 8192], P('ctx', 'tp'), may hold values from -6 to 6
- filters: bfloat16 [128, 8192], P(None, 'tp'), may hold values from -6 to 6, as said below
- norm_gain: float32 [8192], P('tp'), may hold values from 0.1 to 1.9
- grad_out: bfloat16 [2048, 8192], P('ctx', 'tp'), may hold values from -6 to 6
Outputs:
- mixed: bfloat16 [2048, 8192], P('ctx', 'tp')
- grad_query: bfloat16 [2048, 8192], P('ctx', 'tp')
- grad_key: bfloat16 [2048, 8192], P('ctx', 'tp')
- grad_value: bfloat16 [2048, 8192], P('ctx', 'tp')
- grad_filter: float32 [128, 8192], P(None, 'tp')
- grad_gain: float32 [8192], P('tp')
Inputs may be any that keep to these rules, and one draw needn't show every extreme that they name: `query_proj`: finite real values. `filters`: finite real values.
All inputs are finite; a program needn't handle non-finite values.
Results may differ from a plain program's by a relative error of at most 0.0051.
Values may be sent and summed in bfloat16 or wider, within the bound.
A program may use at most 64 MiB of HBM per device.

v0:
```python
import math
import jax
import jax.numpy as jnp
import numpy as np
from jax import lax
from jax.sharding import PartitionSpec as P

EPS = 1e-06
F32 = jnp.float32
BF16 = jnp.bfloat16


def passed_along(array, axis, by):
    length = lax.axis_size(axis)
    pairs = [(i, i + by) for i in range(length) if 0 <= i + by < length]
    return lax.ppermute(array, axis, pairs)


def split(array):
    high = array.astype(BF16)
    return (high, (array - high.astype(array.dtype)).astype(BF16))


def dft_matrices(block):
    length = 2 * block
    freq = np.concatenate([np.arange(0, block, 2), np.arange(1, block, 2)])
    at = np.arange(block)
    angle = 2.0 * np.pi * (freq[:, None] * at[None, :] % length) / length
    sign = np.where(at % 2 == 0, 1.0, -1.0)
    real, imag = (np.cos(angle), -np.sin(angle))
    imag[0] = sign
    forward = np.concatenate([real, imag], 0)
    back = np.concatenate([2.0 * real, 2.0 * imag], 0)
    back[0] *= 0.5
    back[block] *= 0.5
    back = back.T / length

    def parts(matrix):
        matrix = matrix.astype(np.float32)
        high = matrix.astype(jnp.bfloat16)
        low = (matrix - high.astype(np.float32)).astype(jnp.bfloat16)
        return (high, low)

    fh, fl = parts(forward)
    bh, bl = parts(back)
    return (np.concatenate([fh, fl], 1), np.concatenate([bh, bl, bh], 1))


def flip(spec):
    quarter = spec.shape[0] // 4
    return jnp.concatenate(
        [
            spec[:quarter],
            -spec[quarter : 2 * quarter],
            spec[2 * quarter : 3 * quarter],
            -spec[3 * quarter :],
        ],
        0,
    )


def product(a, b, conj):
    half = a.shape[0] // 2
    ar, ai, br, bi = (a[:half], a[half:], b[:half], b[half:])
    first = lax.broadcasted_iota(jnp.int32, ar.shape, 0) == 0
    rr, ii = (ar * br, ai * bi)
    if conj:
        real = jnp.where(first, rr, rr + ii)
        imag = jnp.where(first, ii, ai * br - ar * bi)
    else:
        real = jnp.where(first, rr, rr - ii)
        imag = jnp.where(first, ii, ai * br + ar * bi)
    return jnp.concatenate([real, imag], 0)


def on_device(query_proj, key_proj, value_proj, filters, norm_gain, grad_out):
    row_count, col_count = query_proj.shape
    taps = filters.shape[0]
    blocks = row_count // taps
    width = col_count * lax.axis_size("tp")
    scale = 1.0 / math.sqrt(row_count * lax.axis_size("ctx"))
    forward, back = dft_matrices(taps)

    def to_spec(rows):
        return jnp.dot(forward, jnp.concatenate([rows, rows], 0), preferred_element_type=F32)

    def from_spec(spec):
        high, low = split(spec)
        return jnp.dot(back, jnp.concatenate([high, high, low], 0), preferred_element_type=F32)

    key_wide = key_proj.astype(F32)
    value_wide = value_proj.astype(F32)
    query_wide = query_proj.astype(F32)
    key_value = (key_wide * value_wide).astype(BF16)
    before = passed_along(key_value[row_count - taps :], "ctx", 1)
    filt = to_spec(filters)
    kv_spec = [to_spec(before)] + [
        to_spec(key_value[b * taps : (b + 1) * taps]) for b in range(blocks)
    ]
    kv_win = [kv_spec[b + 1] + flip(kv_spec[b]) for b in range(blocks)]
    conv_out = jnp.concatenate([from_spec(product(w, filt, False)) for w in kv_win], 0)
    gated = query_wide * conv_out
    grad_wide = grad_out.astype(F32)
    grad_scaled = grad_wide * norm_gain
    stats = lax.psum(jnp.stack([jnp.sum(gated * gated, 1), jnp.sum(grad_scaled * gated, 1)]), "tp")
    inv_rms = lax.rsqrt(stats[0] / width + EPS)
    row_mean = stats[1] * inv_rms / width
    normed = gated * inv_rms[:, None]
    mixed = (normed * norm_gain).astype(BF16)
    grad_gated = (grad_scaled - normed * row_mean[:, None]) * inv_rms[:, None]
    grad_query = (grad_gated * conv_out).astype(BF16)
    grad_conv = (grad_gated * query_wide).astype(BF16)
    after = passed_along(grad_conv[:taps], "ctx", -1)
    gc_spec = [to_spec(grad_conv[b * taps : (b + 1) * taps]) for b in range(blocks)]
    filter_spec = sum((product(gc_spec[b], kv_win[b], True) for b in range(blocks)))
    filter_local = from_spec(filter_spec)
    gain_local = jnp.sum(grad_wide * normed, 0)
    total = lax.psum(jnp.concatenate([filter_local, gain_local[None]], 0), "ctx") * scale
    gc_spec = gc_spec + [to_spec(after)]
    gc_win = [gc_spec[b] + flip(gc_spec[b + 1]) for b in range(blocks)]
    grad_kv = jnp.concatenate([from_spec(product(w, filt, True)) for w in gc_win], 0)
    grad_key = (grad_kv * value_wide).astype(BF16)
    grad_value = (grad_kv * key_wide).astype(BF16)
    return (mixed, grad_query, grad_key, grad_value, total[:taps], total[taps])


def solution(mesh):
    placed = (
        P("ctx", "tp"),
        P("ctx", "tp"),
        P("ctx", "tp"),
        P(None, "tp"),
        P("tp"),
        P("ctx", "tp"),
    )
    return jax.shard_map(
        on_device,
        mesh=mesh,
        in_specs=placed,
        out_specs=(
            P("ctx", "tp"),
            P("ctx", "tp"),
            P("ctx", "tp"),
            P("ctx", "tp"),
            P(None, "tp"),
            P("tp"),
        ),
        check_vma=False,
    )
```

profile of v0, /device:TPU:0, one launch (start us, length us, event | category | flops | bytes accessed | tf_op | source)
XLA Modules:
  0.0 159.9 jit_solution(13736018145283497802)
XLA Ops:
  7.2 2.0 %fusion.18 = bf16[256,2048]{1,0:T(8,128)(2,1)S(1)} fusion(bf16[256,2048]{1,0:T(8,128)(2,1)} %param.10, bf16[256,2048]{1,0:T(8,128)(2,1)} %param.9), kind=kLoop, calls=%fused_computation.42 | loop fusion | flops 2097152 | bytes 3145728 | tf_op jit(solution)/shard_map/convert_element_type | solution.py:94
  9.3 4.9 %collective-permute-start = (bf16[128,2048]{1,0:T(8,128)(2,1)S(1)}, bf16[128,2048]{1,0:T(8,128)(2,1)S(1)}, u32[]{:S(2)}, u32[]{:S(2)}) collective-permute-start(bf16[128,2048]{1,0:T(8,128)(2,1)S(1)} %slice.194), channel_id=1, source_target_pairs={{0,4},{4,8},{8,12},{12,16},{16,20},{20,24},{24,28},{1,5},{5,9},{9,... | collective-permute-start | bytes 1572872 | tf_op jit(solution)/shard_map/ppermute | solution.py:16
  16.0 9.4 %collective-permute-done = bf16[128,2048]{1,0:T(8,128)(2,1)S(1)} collective-permute-done((bf16[128,2048]{1,0:T(8,128)(2,1)S(1)}, bf16[128,2048]{1,0:T(8,128)(2,1)S(1)}, u32[]{:S(2)}, u32[]{:S(2)}) %collective-permute-start) | collective-permute-done | bytes 524320 | tf_op jit(solution)/shard_map/ppermute | solution.py:16
  26.3 0.7 maximum_add_fusion
  27.7 1.0 subtract_select_fusion.1
  31.6 1.0 copy-done.6
  33.1 0.7 multiply_reduce_fusion
  33.8 5.7 %psum.14 = f32[2,256]{1,0:T(2,128)S(1)} all-reduce(f32[2,256]{1,0:T(2,128)S(1)} %pad_maximum_fusion.7), channel_id=1, replica_groups=mesh['ctx'=8,'tp'=4] {'tp'}, use_global_device_ids=true, to_apply=%region_2.3 | all-reduce | flops 512 | bytes 4096 | tf_op jit(solution)/shard_map/psum | solution.py:105
  39.6 4.5 %fusion.16 = (bf16[256,2048]{1,0:T(8,128)(2,1)S(1)}, bf16[256,2048]{1,0:T(8,128)(2,1)}, f32[2048]{0:T(1024)S(1)}, bf16[256,2048]{1,0:T(8,128)(2,1)}) fusion(bf16[256,2048]{1,0:T(8,128)(2,1)} %param.8, f32[256]{0:T(256)S(1)} %multiply_multiply_fusion, f32[256]{0:T(256)S(1)} %bitcast.69, f32[2048]{0:T(1024)S(1)} %copy-done.15, bf16[256,2048]{1,0:T(8,128)(2,1)} %param.13, ...), kind=kLoop, calls=%fused_computation.40 | loop fusion | flops 8910848 | bytes 7358464 | tf_op jit(solution)/shard_map/convert_element_type | solution.py:112
  44.1 1.5 collective-permute-start.1
  46.5 14.0 %collective-permute-done.1 = bf16[128,2048]{1,0:T(8,128)(2,1)S(1)} collective-permute-done((bf16[128,2048]{1,0:T(8,128)(2,1)S(1)}, bf16[128,2048]{1,0:T(8,128)(2,1)S(1)}, u32[]{:S(2)}, u32[]{:S(2)}) %collective-permute-start.1) | collective-permute-done | bytes 524320 | tf_op jit(solution)/shard_map/ppermute | solution.py:16
  61.5 1.8 %maximum_add_fusion.2 = (f32[256,2048]{1,0:T(8,128)}, f32[256,2048]{1,0:T(8,128)S(1)}) fusion(f32[64,2048]{1,0:T(8,128)S(1)} %get-tuple-element.35, f32[64,2048]{1,0:T(8,128)S(1)} %get-tuple-element.36, f32[64,2048]{1,0:T(8,128)S(1)} %get-tuple-element.37, f32[64,2048]{1,0:T(8,128)S(1)} %get-tuple-element.34, f32[2048,256]{0,1:T(8,128)S(1)} %fusion.26, ...), kind=kOutput, calls=%fused_computation.51 | convolution fusion | flops 136839168 | bytes 8978432 | tf_op jit(solution)/shard_map/dot_general | solution.py:85
  63.5 1.8 %maximum_add_fusion.1 = (f32[256,2048]{1,0:T(8,128)}, f32[256,2048]{1,0:T(8,128)S(1)}) fusion(f32[64,2048]{1,0:T(8,128)S(1)} %get-tuple-element.31, f32[64,2048]{1,0:T(8,128)S(1)} %get-tuple-element.32, f32[64,2048]{1,0:T(8,128)S(1)} %get-tuple-element.33, f32[64,2048]{1,0:T(8,128)S(1)} %get-tuple-element.30, f32[2048,256]{0,1:T(8,128)S(1)} %fusion.64, ...), kind=kOutput, calls=%fused_computation.49 | convolution fusion | flops 136839168 | bytes 8978432 | tf_op jit(solution)/shard_map/dot_general | solution.py:85
  65.4 1.2 add_select_fusion.1
  67.6 0.7 fusion.9
  68.3 1.2 pad_maximum_fusion.6
  69.5 0.8 copy-done.5
  70.3 3.0 %add_select_fusion.3 = (f32[128,2048]{1,0:T(8,128)S(1)}, f32[128,2048]{1,0:T(8,128)S(1)}, f32[128,2048]{1,0:T(8,128)S(1)}, f32[128,2048]{1,0:T(8,128)S(1)}) fusion(f32[256,2048]{1,0:T(8,128)} %get-tuple-element.52, f32[256,2048]{1,0:T(8,128)S(1)} %copy-done.5, pred[128]{0:T(512)(128)(4,1)S(1)} %iota_compare_fusion, f32[256,2048]{1,0:T(8,128)} %get-tuple-element.54), kind=kLoop, calls=%fused_computation.70 | loop fusion | flops 4194304 | bytes 10485888 | tf_op jit(solution)/shard_map/jit(_where)/select_n | solution.py:68
  75.2 0.9 copy-done.8
  76.4 1.9 %fusion.17 = (bf16[256,2048]{1,0:T(8,128)(2,1)}, bf16[256,2048]{1,0:T(8,128)(2,1)}) fusion(bf16[256,2048]{1,0:T(8,128)(2,1)S(1)} %copy-done.9, f32[128,2048]{1,0:T(8,128)S(1)} %fusion.10, f32[128,2048]{1,0:T(8,128)S(1)} %fusion.11, bf16[256,2048]{1,0:T(8,128)(2,1)S(1)} %copy-done.8), kind=kLoop, calls=%fused_computation.41 | loop fusion | flops 3670016 | bytes 6291456 | tf_op jit(solution)/shard_map/convert_element_type | solution.py:123
  78.3 71.7 %all-reduce.2.cloned.1.call-done = f32[129,2048]{1,0:T(8,128)} async-done(((f32[129,2048]{1,0:T(8,128)}), f32[129,2048]{1,0:T(8,128)}) %all-reduce.2.cloned.1.call-update) | async-done | bytes 1056784 | tf_op jit(solution)/shard_map/psum | solution.py:118
  150.1 1.4 broadcast_multiply_fusion
  151.4 0.6 slice.230
  152.0 1.1 slice.229
  (67 shorter events, 12.3 us)
Async XLA Ops:
  7.2 7.9 %copy-start = (bf16[128,2048]{1,0:T(8,128)(2,1)S(1)}, bf16[128,2048]{1,0:T(8,128)(2,1)}, u32[]{:S(2)}) copy-start(bf16[128,2048]{1,0:T(8,128)(2,1)} %param.11) | copy-start | bytes 1572868
  7.2 7.0 %copy-start.13 = (bf16[256,128]{1,0:T(8,128)(2,1)S(1)}, bf16[256,128]{1,0:T(8,128)(2,1)}, u32[]{:S(2)}) copy-start(bf16[256,128]{1,0:T(8,128)(2,1)} %constant.18) | copy-start | bytes 196612
  7.2 142.9 %all-reduce.2.cloned.1.call-start = ((), (), s32[]{:S(2)}) async-start(), calls=%async_computation | async-start | bytes 2228224 | tf_op jit(solution)/shard_map/psum | solution.py:118
  9.3 16.0 %collective-permute-start = (bf16[128,2048]{1,0:T(8,128)(2,1)S(1)}, bf16[128,2048]{1,0:T(8,128)(2,1)S(1)}, u32[]{:S(2)}, u32[]{:S(2)}) collective-permute-start(bf16[128,2048]{1,0:T(8,128)(2,1)S(1)} %slice.194), channel_id=1, source_target_pairs={{0,4},{4,8},{8,12},{12,16},{16,20},{20,24},{24,28},{1,5},{5,9},{9,... | collective-permute-start | bytes 1572872 | tf_op jit(solution)/shard_map/ppermute | solution.py:16
  14.6 0.9 copy-start.12
  15.9 11.7 %copy-start.4 = (f32[256,2048]{1,0:T(8,128)}, f32[256,2048]{1,0:T(8,128)S(1)}, u32[]{:S(2)}) copy-start(f32[256,2048]{1,0:T(8,128)S(1)} %convolution_add_fusion.6) | copy-start | bytes 6291460
  27.6 1.4 copy-start.2
  27.7 1.4 copy-start.7
  29.1 0.8 copy-start.14
  31.2 1.3 copy-start.10
  31.2 1.9 %copy-start.11 = (bf16[256,2048]{1,0:T(8,128)(2,1)S(1)}, bf16[256,2048]{1,0:T(8,128)(2,1)}, u32[]{:S(2)}) copy-start(bf16[256,2048]{1,0:T(8,128)(2,1)} %param.13) | copy-start | bytes 3145732
  31.2 1.9 %copy-start.15 = (f32[2048]{0:T(1024)S(1)}, f32[2048]{0:T(1024)}, u32[]{:S(2)}) copy-start(f32[2048]{0:T(1024)} %param.12) | copy-start | bytes 24580
  31.6 1.0 copy-start.6
  44.1 16.3 %collective-permute-start.1 = (bf16[128,2048]{1,0:T(8,128)(2,1)S(1)}, bf16[128,2048]{1,0:T(8,128)(2,1)S(1)}, u32[]{:S(2)}, u32[]{:S(2)}) collective-permute-start(bf16[128,2048]{1,0:T(8,128)(2,1)S(1)} %slice.211), channel_id=1, source_target_pairs={{4,0},{8,4},{12,8},{16,12},{20,16},{24,20},{28,24},{5,1},{9,5},{13... | collective-permute-start | bytes 1572872 | tf_op jit(solution)/shard_map/ppermute | solution.py:16
  63.5 1.9 %copy-start.3 = (f32[256,2048]{1,0:T(8,128)S(1)}, f32[256,2048]{1,0:T(8,128)}, u32[]{:S(2)}) copy-start(f32[256,2048]{1,0:T(8,128)} %copy-done.2) | copy-start | bytes 6291460
  68.3 2.0 %copy-start.5 = (f32[256,2048]{1,0:T(8,128)S(1)}, f32[256,2048]{1,0:T(8,128)}, u32[]{:S(2)}) copy-start(f32[256,2048]{1,0:T(8,128)} %copy-done.4) | copy-start | bytes 6291460
  74.9 1.2 copy-start.8
  74.9 1.5 copy-start.9
  76.4 76.7 %copy-start.1 = (bf16[128,2048]{1,0:T(8,128)(2,1)S(1)}, bf16[128,2048]{1,0:T(8,128)(2,1)}, u32[]{:S(2)}) copy-start(bf16[128,2048]{1,0:T(8,128)(2,1)} %param.11) | copy-start | bytes 1572868
Sparse Core Ops, SparseCore 0:
  69.6 80.3 all-reduce.1
where the time goes:
time: 160 us
  waiting for transfers between devices  95.1 us (59%)
  other arithmetic  17.8 us (11%)
  between operations  14.5 us (9%)
  matrix products  14.1 us (9%)
  starting transfers between devices  6.41 us (4%)
  local copies, waits for them, and re-layouts  6.36 us (4%)
  blocking collectives  5.71 us (4%)
    psum x1, waiting for transfers between devices, on_device(): lax.psum(jnp.concatenate([filter_local, gain_local[None]], 0), 'ctx')  71.7 us
    ppermute x2, waiting for transfers between devices, passed_along(): return lax.ppermute(array, axis, pairs)  23.3 us
    dot_general x14, matrix products, to_spec(): jnp.dot(forward, jnp.concatenate([rows, rows], 0), preferred_element_type...  8.98 us
    ppermute x2, starting transfers between devices, passed_along(): return lax.ppermute(array, axis, pairs)  6.38 us
    psum x1, blocking collectives, on_device(): lax.psum(jnp.stack([jnp.sum(gated * gated, 1), jnp.sum(grad_scaled * gate...  5.71 us
    dot_general x15, matrix products, from_spec(): jnp.dot(back, jnp.concatenate([high, high, low], 0), preferred_element_ty...  5.13 us
    unnamed x32, local copies, waits for them, and re-layouts  4.61 us
    convert_element_type x1, other arithmetic, on_device(): grad_conv = (grad_gated * query_wide).astype(BF16)  4.54 us
  transfers between devices with their start and end apart: 3, of which 3 were waited for; matrix products, arithmetic and copies ran while one was open for 6% of the time, Pallas kernels for 0%

commit v1 on v0

--- a/solution.py
+++ b/solution.py
@@ -115,7 +115,10 @@
     filter_spec = sum((product(gc_spec[b], kv_win[b], True) for b in range(blocks)))
     filter_local = from_spec(filter_spec)
     gain_local = jnp.sum(grad_wide * normed, 0)
-    total = lax.psum(jnp.concatenate([filter_local, gain_local[None]], 0), "ctx") * scale
+    total = (
+        jnp.sum(lax.all_gather(jnp.concatenate([filter_local, gain_local[None]], 0), "ctx"), axis=0)
+        * scale
+    )
     gc_spec = gc_spec + [to_spec(after)]
     gc_win = [gc_spec[b] + flip(gc_spec[b + 1]) for b in range(blocks)]
     grad_kv = jnp.concatenate([from_spec(product(w, filt, True)) for w in gc_win], 0)

time: 160 us -> 216 us (1.35)
  waiting for transfers between devices: 95.1 us -> 148 us
  other arithmetic: 17.8 us -> 21 us
    all_gather x0 -> x1, waiting for transfers between devices: none -> 124 us  [on_device(): lax.all_gather(jnp.concatenate([filter_local, gain_local[None]], 0), 'ctx')]
    psum x1 -> x0, waiting for transfers between devices: 71.7 us -> none  [on_device(): lax.psum(jnp.concatenate([filter_local, gain_local[None]], 0), 'ctx')]
    reduce_sum x0 -> x1, other arithmetic: none -> 4.55 us  [on_device(): jnp.sum(lax.all_gather(jnp.concatenate([filter_local, gain_local[None]],...]
  transfers between devices with their start and end apart: 3 -> 3, of which waited for: 3 -> 3; matrix products, arithmetic and copies ran while one was open for 6% -> 4% of each run, Pallas kernels for 0% -> 0%
where the time goes in v1:
time: 216 us
  waiting for transfers between devices  148 us (69%)
  other arithmetic  21 us (10%)
  between operations  14.4 us (7%)
  matrix products  14.2 us (7%)
  local copies, waits for them, and re-layouts  6.45 us (3%)
  starting transfers between devices  6.41 us (3%)
  blocking collectives  5.71 us (3%)
    all_gather x1, waiting for transfers between devices, on_device(): lax.all_gather(jnp.concatenate([filter_local, gain_local[None]], 0), 'ctx')  124 us
    ppermute x2, waiting for transfers between devices, passed_along(): return lax.ppermute(array, axis, pairs)  23.3 us
    dot_general x14, matrix products, to_spec(): jnp.dot(forward, jnp.concatenate([rows, rows], 0), preferred_element_type...  9.04 us
    ppermute x2, starting transfers between devices, passed_along(): return lax.ppermute(array, axis, pairs)  6.38 us
    psum x1, blocking collectives, on_device(): lax.psum(jnp.stack([jnp.sum(gated * gated, 1), jnp.sum(grad_scaled * gate...  5.71 us
    dot_general x15, matrix products, from_spec(): jnp.dot(back, jnp.concatenate([high, high, low], 0), preferred_element_ty...  5.15 us
    unnamed x32, local copies, waits for them, and re-layouts  4.7 us
    reduce_sum x1, other arithmetic, on_device(): jnp.sum(lax.all_gather(jnp.concatenate([filter_local, gain_local[None]],...  4.55 us
  transfers between devices with their start and end apart: 3, of which 3 were waited for; matrix products, arithmetic and copies ran while one was open for 4% of the time, Pallas kernels for 0%

profile of v1, /device:TPU:0, one launch (start us, length us, event | category | flops | bytes accessed | tf_op | source)
XLA Modules:
  0.0 215.9 jit_solution(8109991458813567092)
XLA Ops:
  7.2 2.0 fusion.18
  9.3 4.9 %collective-permute-start = (bf16[128,2048]{1,0:T(8,128)(2,1)S(1)}, bf16[128,2048]{1,0:T(8,128)(2,1)S(1)}, u32[]{:S(2)}, u32[]{:S(2)}) collective-permute-start(bf16[128,2048]{1,0:T(8,128)(2,1)S(1)} %slice.194), channel_id=1, source_target_pairs={{0,4},{4,8},{8,12},{12,16},{16,20},{20,24},{24,28},{1,5},{5,9},{9,... | collective-permute-start | bytes 1572872 | tf_op jit(solution)/shard_map/ppermute | solution.py:16
  16.0 9.4 %collective-permute-done = bf16[128,2048]{1,0:T(8,128)(2,1)S(1)} collective-permute-done((bf16[128,2048]{1,0:T(8,128)(2,1)S(1)}, bf16[128,2048]{1,0:T(8,128)(2,1)S(1)}, u32[]{:S(2)}, u32[]{:S(2)}) %collective-permute-start) | collective-permute-done | bytes 524320 | tf_op jit(solution)/shard_map/ppermute | solution.py:16
  26.3 0.7 maximum_add_fusion
  27.7 1.0 subtract_select_fusion.1
  31.6 1.0 copy-done.6
  33.1 0.7 multiply_reduce_fusion
  33.8 5.7 %psum.7 = f32[2,256]{1,0:T(2,128)S(1)} all-reduce(f32[2,256]{1,0:T(2,128)S(1)} %pad_maximum_fusion.6), channel_id=1, replica_groups=mesh['ctx'=8,'tp'=4] {'tp'}, use_global_device_ids=true, to_apply=%region_2.3 | all-reduce | flops 512 | bytes 4096 | tf_op jit(solution)/shard_map/psum | solution.py:105
  39.6 4.5 %fusion.16 = (bf16[256,2048]{1,0:T(8,128)(2,1)S(1)}, bf16[256,2048]{1,0:T(8,128)(2,1)}, f32[2048]{0:T(1024)S(1)}, bf16[256,2048]{1,0:T(8,128)(2,1)}) fusion(bf16[256,2048]{1,0:T(8,128)(2,1)} %param.8, f32[256]{0:T(256)S(1)} %multiply_multiply_fusion, f32[256]{0:T(256)S(1)} %bitcast.71, f32[2048]{0:T(1024)S(1)} %copy-done.15, bf16[256,2048]{1,0:T(8,128)(2,1)} %param.13, ...), kind=kLoop, calls=%fused_computation.40 | loop fusion | flops 8910848 | bytes 7358464 | tf_op jit(solution)/shard_map/convert_element_type | solution.py:112
  44.1 1.5 collective-permute-start.1
  46.5 14.0 %collective-permute-done.1 = bf16[128,2048]{1,0:T(8,128)(2,1)S(1)} collective-permute-done((bf16[128,2048]{1,0:T(8,128)(2,1)S(1)}, bf16[128,2048]{1,0:T(8,128)(2,1)S(1)}, u32[]{:S(2)}, u32[]{:S(2)}) %collective-permute-start.1) | collective-permute-done | bytes 524320 | tf_op jit(solution)/shard_map/ppermute | solution.py:16
  61.5 1.9 maximum_add_fusion.2
  63.6 1.8 maximum_add_fusion.1
  65.4 1.2 add_select_fusion.1
  67.6 0.7 fusion.9
  68.4 1.1 maximum_bitcast_fusion
  69.5 0.9 copy-done.5
  70.3 3.0 %add_select_fusion.3 = (f32[128,2048]{1,0:T(8,128)S(1)}, f32[128,2048]{1,0:T(8,128)S(1)}, f32[128,2048]{1,0:T(8,128)S(1)}, f32[128,2048]{1,0:T(8,128)S(1)}) fusion(f32[256,2048]{1,0:T(8,128)} %get-tuple-element.52, f32[256,2048]{1,0:T(8,128)S(1)} %copy-done.5, pred[128]{0:T(512)(128)(4,1)S(1)} %iota_compare_fusion, f32[256,2048]{1,0:T(8,128)} %get-tuple-element.54), kind=kLoop, calls=%fused_computation.70 | loop fusion | flops 4194304 | bytes 10485888 | tf_op jit(solution)/shard_map/jit(_where)/select_n | solution.py:68
  75.3 0.9 copy-done.8
  76.5 1.9 fusion.17
  78.4 124.3 %all-gather.4.cloned.1.call-done = f32[8,129,2048]{2,1,0:T(8,128)} async-done(((f32[1,129,2048]{2,1,0:T(8,128)}), f32[8,129,2048]{2,1,0:T(8,128)}) %all-gather.4.cloned.1.call-update) | async-done | bytes 8454160 | tf_op jit(solution)/shard_map/all_gather | solution.py:119
  202.7 4.5 %reduce_sum.39 = f32[129,2048]{1,0:T(8,128)S(1)} reduce(f32[8,129,2048]{2,1,0:T(8,128)} %all-gather.4.cloned.1.call-done, f32[]{:T(128)} %constant.5.clone.1), dimensions={0}, to_apply=%region_4.5 | reduce | flops 1849344 | bytes 9510916 | tf_op jit(solution)/shard_map/reduce_sum | solution.py:119
  207.4 0.6 slice.230
  208.0 1.1 slice.229
  (68 shorter events, 12.4 us)
Async XLA Ops:
  7.2 7.9 %copy-start = (bf16[128,2048]{1,0:T(8,128)(2,1)S(1)}, bf16[128,2048]{1,0:T(8,128)(2,1)}, u32[]{:S(2)}) copy-start(bf16[128,2048]{1,0:T(8,128)(2,1)} %param.11) | copy-start | bytes 1572868
  7.2 7.0 %copy-start.13 = (bf16[256,128]{1,0:T(8,128)(2,1)S(1)}, bf16[256,128]{1,0:T(8,128)(2,1)}, u32[]{:S(2)}) copy-start(bf16[256,128]{1,0:T(8,128)(2,1)} %constant.18) | copy-start | bytes 196612
  7.2 195.5 %all-gather.4.cloned.1.call-start = ((), (), s32[]{:S(2)}) async-start(), calls=%async_computation | async-start | bytes 10027008 | tf_op jit(solution)/shard_map/all_gather | solution.py:119
  9.3 16.0 %collective-permute-start = (bf16[128,2048]{1,0:T(8,128)(2,1)S(1)}, bf16[128,2048]{1,0:T(8,128)(2,1)S(1)}, u32[]{:S(2)}, u32[]{:S(2)}) collective-permute-start(bf16[128,2048]{1,0:T(8,128)(2,1)S(1)} %slice.194), channel_id=1, source_target_pairs={{0,4},{4,8},{8,12},{12,16},{16,20},{20,24},{24,28},{1,5},{5,9},{9,... | collective-permute-start | bytes 1572872 | tf_op jit(solution)/shard_map/ppermute | solution.py:16
  14.6 0.9 copy-start.12
  15.9 11.7 %copy-start.4 = (f32[256,2048]{1,0:T(8,128)}, f32[256,2048]{1,0:T(8,128)S(1)}, u32[]{:S(2)}) copy-start(f32[256,2048]{1,0:T(8,128)S(1)} %convolution_add_fusion.6) | copy-start | bytes 6291460
  27.6 1.4 copy-start.2
  27.7 1.4 copy-start.7
  29.1 0.8 copy-start.14
  31.2 1.3 copy-start.10
  31.2 1.9 copy-start.11
  31.2 1.9 copy-start.15
  31.6 1.0 copy-start.6
  44.1 16.3 %collective-permute-start.1 = (bf16[128,2048]{1,0:T(8,128)(2,1)S(1)}, bf16[128,2048]{1,0:T(8,128)(2,1)S(1)}, u32[]{:S(2)}, u32[]{:S(2)}) collective-permute-start(bf16[128,2048]{1,0:T(8,128)(2,1)S(1)} %slice.211), channel_id=1, source_target_pairs={{4,0},{8,4},{12,8},{16,12},{20,16},{24,20},{28,24},{5,1},{9,5},{13... | collective-permute-start | bytes 1572872 | tf_op jit(solution)/shard_map/ppermute | solution.py:16
  63.6 1.9 copy-start.3
  68.3 2.0 copy-start.5
  74.9 1.2 copy-start.8
  75.0 1.5 copy-start.9
  202.7 6.3 %copy-start.1 = (bf16[128,2048]{1,0:T(8,128)(2,1)S(1)}, bf16[128,2048]{1,0:T(8,128)(2,1)}, u32[]{:S(2)}) copy-start(bf16[128,2048]{1,0:T(8,128)(2,1)} %param.11) | copy-start | bytes 1572868
Sparse Core Ops, SparseCore 0:
  69.6 133.0 all-gather.3
